TPU v7x, 512 devices: a whole 4x4x16 slice. The times are simulated.
512 devices in a mesh: fsdp: 2 (over z_hi), seq: 32 (over x, y, core), tp: 8 (over z_lo).
Axes of the slice: x: 4, y: 4, z: 16 (z_hi: 2, z_lo: 8; z = z_hi * 8 + z_lo), core: 2. Of those that a mesh axis runs over, the one named last changes fastest.
Arguments:
- tokens: bfloat16 [16384, 8192], P(('fsdp', 'seq', 'tp')), may hold values from -6 to 6
- proj_mean: bfloat16 [8192, 4096], P(('fsdp', 'seq'), 'tp'), may hold values from -0.0625 to 0.0625
- proj_devs: bfloat16 [4, 8192, 4096], P(None, ('fsdp', 'seq'), 'tp'), may hold values from -0.0625 to 0.0625
- bc_mean: bfloat16 [8192, 2, 1024], P(('fsdp', 'seq'), None, 'tp'), may hold values from -0.0625 to 0.0625
- bc_devs: bfloat16 [4, 8192, 2, 1024], P(None, ('fsdp', 'seq'), None, 'tp'), may hold values from -0.0625 to 0.0625
- swag_coef: float32 [4], replicated, may hold values from -4 to 4
- dt_weight: bfloat16 [8192, 64], P(('fsdp', 'seq'), 'tp'), may hold values from -0.0625 to 0.0625
- dt_bias: float32 [64], P('tp'), may hold values from -12 to -2, as said below
- decay_rate: float32 [64], P('tp'), may hold values from 0 to 16, as said below
- skip_gain: float32 [64], P('tp'), may hold values from 0.5 to 1.5
- conv_proj: float32 [4, 4096], P(None, 'tp'), may hold values from -3 to 3
- conv_bc: float32 [4, 2, 1024], P(None, None, 'tp'), may hold values from -1.5 to 1.5
Outputs:
- ssm_out: bfloat16 [16384, 4096], P(('fsdp', 'seq'), 'tp')
Inputs may be any that keep to these rules, and one draw needn't show every extreme that they name: `dt_bias`: every bias is the inverse softplus of a positive step size. `decay_rate`: every rate is positive.
All inputs are finite; a program needn't handle non-finite values.
Results may differ from a plain program's by a relative error of at most 0.0059.
Values may be sent and summed in bfloat16 or wider, within the bound.
A program may use at most 64 MiB of HBM per device.

v0:
```python
import jax
import jax.numpy as jnp
from jax import lax
from jax.sharding import PartitionSpec as P

P_SIZE = 64
N = 128
CONV = 4
SPAN = 128


def shifted(shard, axis, by):
    count = lax.axis_size(axis)
    pairs = [(i, i + by) for i in range(count) if 0 <= i + by < count]
    return lax.ppermute(shard, axis, pairs)


def prefix(part, axis, combine, identity):
    place = lax.axis_index(axis)
    gathered = jax.tree.map(lambda a: lax.all_gather(a, axis), part)
    state = jax.tree.map(lambda a, e: jnp.zeros_like(a) + jnp.asarray(e, a.dtype), part, identity)

    def one(hop, state):
        return combine(
            state, jax.tree.map(lambda a: lax.dynamic_index_in_dim(a, hop, 0, False), gathered)
        )

    return lax.fori_loop(0, place, one, state)


def sampled(mean_part, dev_part, swag_coef):
    factor = (2.0 * (dev_part.shape[0] - 1)) ** (-0.5)
    accum = mean_part.astype(jnp.float32)
    for member in range(dev_part.shape[0]):
        accum = accum + factor * swag_coef[member] * dev_part[member].astype(jnp.float32)
    return accum.astype(jnp.bfloat16)


def combine(former, latter):
    return (former[0] * latter[0], latter[0][:, None, None] * former[1] + latter[1])


def body(
    tokens,
    proj_mean,
    proj_devs,
    bc_mean,
    bc_devs,
    swag_coef,
    dt_weight,
    dt_bias,
    decay_rate,
    skip_gain,
    conv_proj,
    conv_bc,
):
    heads_here = decay_rate.shape[0]
    groups_here = bc_mean.shape[2] // N
    width_x = proj_mean.shape[1]
    width_bc = 2 * bc_mean.shape[2]
    rows_all = lax.all_gather(tokens, "tp", axis=0, tiled=True)
    tok_count = rows_all.shape[0]
    weight_x = sampled(proj_mean, proj_devs, swag_coef)
    weight_bc = sampled(bc_mean, bc_devs, swag_coef).reshape(bc_mean.shape[0], width_bc)
    weight_all = jnp.concatenate([weight_x, weight_bc], axis=1)
    projected = jnp.dot(
        rows_all,
        lax.all_gather(weight_all, ("fsdp", "seq"), axis=0, tiled=True),
        preferred_element_type=jnp.float32,
    ).astype(jnp.bfloat16)
    step_size = jax.nn.softplus(
        jnp.dot(
            rows_all,
            lax.all_gather(dt_weight, ("fsdp", "seq"), axis=0, tiled=True),
            preferred_element_type=jnp.float32,
        )
        + dt_bias
    )
    rim_rows = shifted(projected[tok_count - (CONV - 1) :], "seq", 1)
    padded = jnp.concatenate([rim_rows, projected], axis=0).astype(jnp.float32)
    kernel = jnp.concatenate([conv_proj, conv_bc.reshape(CONV, width_bc)], axis=1)
    conv_sum = kernel[0] * padded[0:tok_count]
    for offset in range(1, CONV):
        conv_sum = conv_sum + kernel[offset] * padded[offset : offset + tok_count]
    conved = jax.nn.silu(conv_sum).astype(jnp.bfloat16)
    blocks = tok_count // SPAN
    per_group = heads_here // groups_here
    values = conved[:, :width_x].reshape(blocks, SPAN, heads_here, P_SIZE)
    keys_b = conved[:, width_x : width_x + width_bc // 2].reshape(blocks, SPAN, groups_here, N)
    reads_c = conved[:, width_x + width_bc // 2 :].reshape(blocks, SPAN, groups_here, N)
    steps_b = step_size.reshape(blocks, SPAN, heads_here)
    cum_log = jnp.cumsum(-steps_b * decay_rate, axis=1)
    last_cum = cum_log[:, SPAN - 1 :, :]
    scaled = (
        values.astype(jnp.float32) * (jnp.exp(last_cum - cum_log) * steps_b)[..., None]
    ).astype(jnp.bfloat16)
    keys_h = jnp.repeat(keys_b, per_group, axis=2)
    states = jnp.einsum("bshn,bshp->bhnp", keys_h, scaled, preferred_element_type=jnp.float32)
    block_decay = jnp.exp(last_cum[:, 0, :])
    total_decay = block_decay[0]
    total_state = states[0]
    member = 1
    total_decay, total_state = combine(
        (total_decay, total_state), (block_decay[member], states[member])
    )
    incoming = prefix(
        (total_decay, total_state),
        "seq",
        combine,
        (jnp.ones((heads_here,), jnp.float32), jnp.zeros((heads_here, N, P_SIZE), jnp.float32)),
    )
    scores = jnp.einsum("bqgn,bsgn->bgqs", reads_c, keys_b, preferred_element_type=jnp.float32)
    scores = jnp.repeat(scores, per_group, axis=1)
    causal_mask = jnp.tril(jnp.ones((SPAN, SPAN), bool))
    later_cum = jnp.transpose(cum_log, (0, 2, 1))
    cum_gaps = later_cum[:, :, :, None] - later_cum[:, :, None, :]
    decays = jnp.where(causal_mask, jnp.exp(jnp.minimum(cum_gaps, 0.0)), 0.0)
    weights = (scores * decays * jnp.transpose(steps_b, (0, 2, 1))[:, :, None, :]).astype(
        jnp.bfloat16
    )
    inner_part = jnp.einsum("bhqs,bshp->bqhp", weights, values, preferred_element_type=jnp.float32)
    carried = incoming[1]
    entering = []
    for member in range(blocks):
        entering.append(carried)
        carried = block_decay[member][:, None, None] * carried + states[member]
    entering_bf = jnp.stack(entering).astype(jnp.bfloat16)
    reads_h = jnp.repeat(reads_c, per_group, axis=2)
    outer_part = jnp.exp(cum_log)[..., None] * jnp.einsum(
        "bqhn,bhnp->bqhp", reads_h, entering_bf, preferred_element_type=jnp.float32
    )
    result = inner_part + outer_part + skip_gain[:, None] * values.astype(jnp.float32)
    return result.reshape(tok_count, width_x).astype(jnp.bfloat16)


def solution(mesh):
    return jax.shard_map(
        body,
        mesh=mesh,
        in_specs=(
            P(("fsdp", "seq", "tp"), None),
            P(("fsdp", "seq"), "tp"),
            P(None, ("fsdp", "seq"), "tp"),
            P(("fsdp", "seq"), None, "tp"),
            P(None, ("fsdp", "seq"), None, "tp"),
            P(),
            P(("fsdp", "seq"), "tp"),
            P("tp"),
            P("tp"),
            P("tp"),
            P(None, "tp"),
            P(None, None, "tp"),
        ),
        out_specs=P(("fsdp", "seq"), "tp"),
        check_vma=False,
    )
```

profile of v0, /device:TPU:31, one launch (start us, length us, event | category | flops | bytes accessed | tf_op | source)
XLA Modules:
  0.0 457.1 jit_solution(740776401347183553)
XLA Ops:
  7.3 1.5 fusion.31
  11.3 1.2 fusion.26
  12.5 1.3 fusion.21
  14.6 148.3 %all_gather.19 = bf16[8192,8]{0,1:T(8,128)(2,1)S(1)} all-gather(bf16[128,8]{0,1:T(8,128)(2,1)} %param.20), channel_id=1, replica_groups=mesh['fsdp'=2,'seq'=32,'tp'=8] {'fsdp','seq'}, dimensions={0}, use_global_device_ids=true | all-gather | bytes 133120 | tf_op jit(solution)/shard_map/all_gather | solution.py:74
  164.3 3.4 compare_select_fusion
  168.1 160.6 %all-gather.5.cloned.1.call-done = bf16[8192,768]{1,0:T(8,128)(2,1)} async-done(((bf16[128,768]{1,0:T(8,128)(2,1)}), bf16[8192,768]{1,0:T(8,128)(2,1)}) %all-gather.5.cloned.1.call-update) | async-done | bytes 12582928 | tf_op jit(solution)/shard_map/all_gather | solution.py:68
  328.8 9.3 %fusion.4 = bf16[256,768]{1,0:T(8,128)(2,1)S(1)} fusion(bf16[256,8192]{1,0:T(8,128)(2,1)} %all-gather.7.cloned.1.call-done, bf16[8192,768]{1,0:T(8,128)(2,1)} %all-gather.5.cloned.1.call-done), kind=kOutput, calls=%fused_computation.10 | convolution fusion | flops 3221422080 | bytes 17170432 | tf_op jit(solution)/shard_map/dot_general | solution.py:66
  338.0 1.3 collective-permute-start
  339.4 1.7 collective-permute-done
  343.6 23.8 %all-gather = f32[32,1,8]{2,1,0:T(1,128)S(1)} all-gather(f32[1,1,8]{2,1,0:T(1,128)S(1)} %get-tuple-element.87), channel_id=1, replica_groups=mesh['fsdp'=2,'seq'=32,'tp'=8] {'seq'}, dimensions={0}, use_global_device_ids=true | all-gather | bytes 1056 | tf_op jit(solution)/shard_map/all_gather | solution.py:20
  367.6 37.6 %all-gather.9.cloned.1.call-done = f32[32,8,128,64]{2,3,1,0:T(8,128)} async-done(((f32[1,8,128,64]{2,3,1,0:T(8,128)}), f32[32,8,128,64]{2,3,1,0:T(8,128)}) %all-gather.9.cloned.1.call-update) | async-done | bytes 8388624 | tf_op jit(solution)/shard_map/all_gather | solution.py:20
  405.2 42.7 %while.12 = (s32[]{:T(128)}, f32[8,128,64]{2,1,0:T(8,128)S(1)}, s32[]{:T(128)}, f32[32,8]{1,0:T(8,128)S(1)}, f32[32,8,128,64]{2,3,1,0:T(8,128)}, /*index=5*/s32[]{:T(128)}, s32[]{:T(128)}, s32[]{:T(128)}) while((s32[]{:T(128)}, f32[8,128,64]{2,1,0:T(8,128)S(1)}, s32[]{:T(128)}, f32[32,8]{1,0:T(8,128)S(1)}, f32[32,8,128,64]{2,3,1,0:T(8,128)}, ...), condition=%wide.region_2.3_spmd, body=%wide.region_1.2_spmd.sunk | while | flops 131077 | bytes 1835231 | solution.py:28
  405.2 1.0 constant_dynamic-slice_fusion.2
  406.6 1.0 constant_dynamic-slice_fusion.2
  408.0 1.0 constant_dynamic-slice_fusion.2
  412.1 1.0 constant_dynamic-slice_fusion.2
  413.5 1.0 constant_dynamic-slice_fusion.2
  414.9 1.0 constant_dynamic-slice_fusion.2
  416.2 1.0 constant_dynamic-slice_fusion.2
  417.6 1.0 constant_dynamic-slice_fusion.2
  424.5 1.0 constant_dynamic-slice_fusion.2
  425.9 1.0 constant_dynamic-slice_fusion.2
  427.3 1.0 constant_dynamic-slice_fusion.2
  428.6 1.0 constant_dynamic-slice_fusion.2
  430.0 1.0 constant_dynamic-slice_fusion.2
  431.4 1.0 constant_dynamic-slice_fusion.2
  438.3 1.0 constant_dynamic-slice_fusion.2
  439.6 1.0 constant_dynamic-slice_fusion.2
  441.0 1.0 constant_dynamic-slice_fusion.2
  442.4 1.0 constant_dynamic-slice_fusion.2
  443.8 1.0 constant_dynamic-slice_fusion.2
  449.6 1.0 reshape.103
  (148 shorter events, 30.4 us)
Async XLA Ops:
  6.5 161.3 %copy-start = (f32[8]{0:T(128)S(1)}, f32[8]{0:T(128)}, u32[]{:S(2)}) copy-start(f32[8]{0:T(128)} %param.22) | copy-start | bytes 100
  6.5 157.7 %all-gather.7.cloned.1.call-start = ((), (), s32[]{:S(2)}) async-start(), calls=%async_computation.1 | async-start | bytes 4718592 | tf_op jit(solution)/shard_map/all_gather | solution.py:61
  7.3 321.5 %all-gather.5.cloned.1.call-start = ((), (), s32[]{:S(2)}) async-start(), calls=%async_computation | async-start | bytes 12779520 | tf_op jit(solution)/shard_map/all_gather | solution.py:68
  14.5 390.6 %all-gather.9.cloned.1.call-start = ((), (), s32[]{:S(2)}) async-start(), calls=%async_computation.2 | async-start | bytes 8650752 | tf_op jit(solution)/shard_map/all_gather | solution.py:20
  338.0 3.1 collective-permute-start
  405.2 43.5 %copy-start.1 = (f32[8]{0:T(128)S(1)}, f32[8]{0:T(128)}, u32[]{:S(2)}) copy-start(f32[8]{0:T(128)} %param.23) | copy-start | bytes 100
Sparse Core Ops, SparseCore 0:
  9.4 109.3 all-gather.6
  123.3 205.4 all-gather.4
  343.6 61.5 all-gather.8
where the time goes:
time: 458 us; the launch traced here: 457 us
  waiting for transfers between devices  201 us (44%)
  blocking collectives  172 us (38%)
  local copies, waits for them, and re-layouts  42.2 us (9%)
  between operations  15.8 us (3%)
  matrix products  14.1 us (3%)
  other arithmetic  9.38 us (2%)
    all_gather x1, waiting for transfers between devices, body(): lax.all_gather(weight_all, ('fsdp', 'seq'), axis=0, tiled=True)  161 us
    all_gather x1, blocking collectives, body(): lax.all_gather(dt_weight, ('fsdp', 'seq'), axis=0, tiled=True)  148 us
    all_gather x1, waiting for transfers between devices, prefix(): gathered = jax.tree.map(lambda a: lax.all_gather(a, axis), part)  37.6 us
    dynamic_slice x62, local copies, waits for them, and re-layouts, one(): lax.dynamic_index_in_dim(a, hop, 0, False)  36.4 us
    all_gather x1, blocking collectives, prefix(): gathered = jax.tree.map(lambda a: lax.all_gather(a, axis), part)  23.8 us
    dot_general x1, matrix products, body(): jnp.dot(rows_all, lax.all_gather(weight_all, ('fsdp', 'seq'), axis=0, til...  9.25 us
  transfers between devices with their start and end apart: 4, of which 3 were waited for; matrix products, arithmetic and copies ran while one was open for 2% of the time, Pallas kernels for 0%

commit v1 on v0

--- a/solution.py
+++ b/solution.py
@@ -65,7 +65,12 @@
     weight_all = jnp.concatenate([weight_x, weight_bc], axis=1)
     projected = jnp.dot(
         rows_all,
-        lax.all_gather(weight_all, ("fsdp", "seq"), axis=0, tiled=True),
+        jnp.concatenate(
+            lax.all_to_all(
+                jnp.stack([weight_all] * lax.axis_size(("fsdp", "seq"))), ("fsdp", "seq"), 0, 0
+            ),
+            axis=0,
+        ),
         preferred_element_type=jnp.float32,
     ).astype(jnp.bfloat16)
     step_size = jax.nn.softplus(

time: 458 us -> 942 us (2.06)
  blocking collectives: 172 us -> 758 us
  waiting for transfers between devices: 201 us -> 71.9 us
  starting transfers between devices: 1.38 us -> 23 us
    all_gather x1, blocking collectives: 148 us -> 739 us  [body(): lax.all_gather(dt_weight, ('fsdp', 'seq'), axis=0, tiled=True)]
    all_gather x1 -> x0, waiting for transfers between devices: 161 us -> none  [body(): lax.all_gather(weight_all, ('fsdp', 'seq'), axis=0, tiled=True)]
    all_gather x1, waiting for transfers between devices: 37.6 us -> 69.5 us  [prefix(): gathered = jax.tree.map(lambda a: lax.all_gather(a, axis), part)]
    all_to_all x0 -> x1, starting transfers between devices: none -> 21.6 us  [body(): lax.all_to_all(jnp.stack([weight_all] * lax.axis_size(('fsdp', 'seq'))),...]
  transfers between devices with their start and end apart: 4 -> 4, of which waited for: 3 -> 2; matrix products, arithmetic and copies ran while one was open for 2% -> 0% of each run, Pallas kernels for 0% -> 0%
where the time goes in v1:
time: 942 us; the launch traced here: 941 us
  blocking collectives  758 us (80%)
  waiting for transfers between devices  71.9 us (8%)
  local copies, waits for them, and re-layouts  46.8 us (5%)
  starting transfers between devices  23 us (2%)
  between operations  16.2 us (2%)
  matrix products  14.1 us (1%)
    all_gather x1, blocking collectives, body(): lax.all_gather(dt_weight, ('fsdp', 'seq'), axis=0, tiled=True)  739 us
    all_gather x1, waiting for transfers between devices, prefix(): gathered = jax.tree.map(lambda a: lax.all_gather(a, axis), part)  69.5 us
    dynamic_slice x62, local copies, waits for them, and re-layouts, one(): lax.dynamic_index_in_dim(a, hop, 0, False)  36.4 us
    all_to_all x1, starting transfers between devices, body(): lax.all_to_all(jnp.stack([weight_all] * lax.axis_size(('fsdp', 'seq'))),...  21.6 us
    all_gather x1, blocking collectives, prefix(): gathered = jax.tree.map(lambda a: lax.all_gather(a, axis), part)  19 us
  transfers between devices with their start and end apart: 4, of which 2 were waited for; matrix products, arithmetic and copies ran while one was open for 0% of the time, Pallas kernels for 0%

profile of v1, /device:TPU:31, one launch (start us, length us, event | category | flops | bytes accessed | tf_op | source)
XLA Modules:
  0.0 940.6 jit_solution(9102103460210869190)
XLA Ops:
  6.5 1.5 fusion.31
  10.5 1.2 fusion.26
  11.7 1.3 fusion.21
  13.1 6.0 stack.11
  19.1 21.6 %all-to-all-start = ((bf16[64,128,768]{2,1,0:T(8,128)(2,1)}), bf16[64,128,768]{2,1,0:T(8,128)(2,1)}, u32[]{:S(2)}, u32[]{:S(2)}) async-start(bf16[64,128,768]{2,1,0:T(8,128)(2,1)} %stack.11), calls=%async_computation | async-start | bytes 25165824 | tf_op jit(solution)/shard_map/all_to_all | solution.py:69
  41.5 739.3 %all_gather.15 = bf16[8192,8]{0,1:T(8,128)(2,1)S(1)} all-gather(bf16[128,8]{0,1:T(8,128)(2,1)S(1)} %copy-done.2), channel_id=1, replica_groups=mesh['fsdp'=2,'seq'=32,'tp'=8] {'fsdp','seq'}, dimensions={0}, use_global_device_ids=true | all-gather | bytes 133120 | tf_op jit(solution)/shard_map/all_gather | solution.py:79
  780.9 3.4 compare_select_fusion
  784.7 9.3 fusion.4
  794.0 1.3 collective-permute-start
  795.4 1.7 collective-permute-done
  799.6 19.0 %all-gather = f32[32,1,8]{2,1,0:T(1,128)S(1)} all-gather(f32[1,1,8]{2,1,0:T(1,128)S(1)} %get-tuple-element.87), channel_id=1, replica_groups=mesh['fsdp'=2,'seq'=32,'tp'=8] {'seq'}, dimensions={0}, use_global_device_ids=true | all-gather | bytes 1056 | tf_op jit(solution)/shard_map/all_gather | solution.py:20
  818.8 69.5 %all-gather.6.cloned.1.call-done = f32[32,8,128,64]{2,3,1,0:T(8,128)} async-done(((f32[1,8,128,64]{2,3,1,0:T(8,128)}), f32[32,8,128,64]{2,3,1,0:T(8,128)}) %all-gather.6.cloned.1.call-update) | async-done | bytes 8388624 | tf_op jit(solution)/shard_map/all_gather | solution.py:20
  888.4 42.7 %while.12 = (s32[]{:T(128)}, f32[8,128,64]{2,1,0:T(8,128)S(1)}, s32[]{:T(128)}, f32[32,8]{1,0:T(8,128)S(1)}, f32[32,8,128,64]{2,3,1,0:T(8,128)}, /*index=5*/s32[]{:T(128)}, s32[]{:T(128)}, s32[]{:T(128)}) while((s32[]{:T(128)}, f32[8,128,64]{2,1,0:T(8,128)S(1)}, s32[]{:T(128)}, f32[32,8]{1,0:T(8,128)S(1)}, f32[32,8,128,64]{2,3,1,0:T(8,128)}, ...), condition=%wide.region_2.3_spmd, body=%wide.region_1.2_spmd.sunk | while | flops 131077 | bytes 1835231 | solution.py:28
  888.4 1.0 constant_dynamic-slice_fusion.2
  889.8 1.0 constant_dynamic-slice_fusion.2
  891.1 1.0 constant_dynamic-slice_fusion.2
  895.3 1.0 constant_dynamic-slice_fusion.2
  896.6 1.0 constant_dynamic-slice_fusion.2
  898.0 1.0 constant_dynamic-slice_fusion.2
  902.1 1.0 constant_dynamic-slice_fusion.2
  903.5 1.0 constant_dynamic-slice_fusion.2
  904.9 1.0 constant_dynamic-slice_fusion.2
  909.0 1.0 constant_dynamic-slice_fusion.2
  910.4 1.0 constant_dynamic-slice_fusion.2
  914.5 1.0 constant_dynamic-slice_fusion.2
  915.9 1.0 constant_dynamic-slice_fusion.2
  917.3 1.0 constant_dynamic-slice_fusion.2
  921.4 1.0 constant_dynamic-slice_fusion.2
  922.8 1.0 constant_dynamic-slice_fusion.2
  924.2 1.0 constant_dynamic-slice_fusion.2
  928.3 1.0 constant_dynamic-slice_fusion.2
  932.7 1.0 reshape.109
  (156 shorter events, 29.3 us)
Async XLA Ops:
  19.1 22.4 %copy-start.2 = (bf16[128,8]{0,1:T(8,128)(2,1)S(1)}, bf16[128,8]{0,1:T(8,128)(2,1)}, u32[]{:S(2)}) copy-start(bf16[128,8]{0,1:T(8,128)(2,1)} %param.20) | copy-start | bytes 6148
  19.1 761.7 %copy-start = (f32[4,512]{1,0:T(4,128)S(1)}, f32[4,512]{1,0:T(4,128)}, u32[]{:S(2)}) copy-start(f32[4,512]{1,0:T(4,128)} %param.24) | copy-start | bytes 24580
  19.1 761.7 %copy-start.1 = (f32[4,2,128]{2,1,0:T(2,128)S(1)}, f32[4,2,128]{2,1,0:T(2,128)}, u32[]{:S(2)}) copy-start(f32[4,2,128]{2,1,0:T(2,128)} %param.25) | copy-start | bytes 12292
  19.1 761.8 %copy-start.3 = (f32[8]{0:T(128)S(1)}, f32[8]{0:T(128)}, u32[]{:S(2)}) copy-start(f32[8]{0:T(128)} %param.21) | copy-start | bytes 100
  19.1 765.4 %copy-start.4 = (f32[8]{0:T(128)S(1)}, f32[8]{0:T(128)}, u32[]{:S(2)}) copy-start(f32[8]{0:T(128)} %param.22) | copy-start | bytes 100
  19.1 765.6 %all-to-all-start = ((bf16[64,128,768]{2,1,0:T(8,128)(2,1)}), bf16[64,128,768]{2,1,0:T(8,128)(2,1)}, u32[]{:S(2)}, u32[]{:S(2)}) async-start(bf16[64,128,768]{2,1,0:T(8,128)(2,1)} %stack.11), calls=%async_computation | async-start | bytes 25165824 | tf_op jit(solution)/shard_map/all_to_all | solution.py:69
  40.7 740.2 %all-gather.4.cloned.1.call-start = ((), (), s32[]{:S(2)}) async-start(), calls=%async_computation.1 | async-start | bytes 4718592 | tf_op jit(solution)/shard_map/all_gather | solution.py:61
  41.4 846.9 %all-gather.6.cloned.1.call-start = ((), (), s32[]{:S(2)}) async-start(), calls=%async_computation.2 | async-start | bytes 8650752 | tf_op jit(solution)/shard_map/all_gather | solution.py:20
  794.0 3.1 collective-permute-start
  888.3 43.4 %copy-start.5 = (f32[8]{0:T(128)S(1)}, f32[8]{0:T(128)}, u32[]{:S(2)}) copy-start(f32[8]{0:T(128)} %param.23) | copy-start | bytes 100
Sparse Core Ops, SparseCore 0:
  43.6 302.9 all-gather.3
  799.5 88.7 all-gather.5
